TPU v7x, 256 devices: a whole 4x4x8 slice. The times are simulated.
256 devices in a mesh: label: 128 (over x, y_lo, z, core), dp: 2 (over y_hi).
Axes of the slice: x: 4, y: 4 (y_hi: 2, y_lo: 2; y = y_hi * 2 + y_lo), z: 8, core: 2. Of those that a mesh axis runs over, the one named last changes fastest.
Arguments:
- queries: bfloat16 [4096, 512], P(('label', 'dp')), may hold values from -9 to 9
- positives: int32 [4096, 8], P(('label', 'dp')), may hold values from -1 to 131071, as said below
- weights: float32 [131072, 512], P('label'), may hold values from -4 to 4
- first_moment: float32 [131072, 512], P('label'), may hold values from -1.8 to 1.8
- second_moment: float32 [131072, 512], P('label'), may hold values from 0.05 to 1
Outputs:
- new_weights: float32 [131072, 512], P('label')
- new_first: float32 [131072, 512], P('label')
- new_second: float32 [131072, 512], P('label')
- query_grads: float32 [2, 4096, 512], P(None, ('label', 'dp'))
Inputs may be any that keep to these rules, and one draw needn't show every extreme that they name: `positives`: each row lists its query's positive label ids (one to 8) first and -1 in the unused slots after them; ids may repeat within a row.
All inputs are finite; a program needn't handle non-finite values.
Results may differ from a plain program's by a relative error of at most 0.0023.
Values may be sent and summed in bfloat16 or wider, within the bound.
No kernel may reach another device: no remote copies, remote signals or barrier semaphores. Data moves between devices by JAX's collectives and lax.ppermute only.
A program may use at most 128 MiB of HBM per device.

v0:
```python
import jax
import jax.numpy as jnp
from jax import lax
from jax.sharding import PartitionSpec as P

STEPS = 2


beta_one = 0.9
beta_two = 0.95
rate = 0.02
decay = 0.1
epsilon = 1e-08
past_steps = 1000


def contract_last(left, right):
    return lax.dot_general(
        left, right, (((1,), (1,)), ((), ())), preferred_element_type=jnp.float32
    )


def contract_first(left, right):
    return lax.dot_general(
        left, right, (((0,), (0,)), ((), ())), preferred_element_type=jnp.float32
    )


def residuals(rows, pos_rows, wb, label_ids):
    logits = contract_last(rows, wb)
    hits = jnp.any(pos_rows[:, :, None] == label_ids[None, None, :], axis=1)
    return (jax.nn.sigmoid(logits) - hits.astype(jnp.float32)).astype(jnp.bfloat16)


def adamw(weight, first, second, grad, count):
    first = beta_one * first + (1.0 - beta_one) * grad
    second = beta_two * second + (1.0 - beta_two) * grad * grad
    first_hat = first / (1.0 - beta_one**count)
    second_hat = second / (1.0 - beta_two**count)
    weight = weight - rate * (first_hat / (jnp.sqrt(second_hat) + epsilon) + decay * weight)
    return (weight, first, second)


def shards(queries, positives, weights, first_moment, second_moment):
    n_label = lax.axis_size("label")
    rows_dev = queries.shape[0]
    lab_dev = weights.shape[0]
    weight, first, second = (weights, first_moment, second_moment)
    group_rows = rows_dev * n_label
    label_ids = lax.axis_index("label") * lab_dev + jnp.arange(lab_dev, dtype=jnp.int32)
    results = []
    for step in range(STEPS):
        wb = weight.astype(jnp.bfloat16)
        grad_acc = jnp.zeros((lab_dev, weight.shape[1]), jnp.float32)
        rows_acc = jnp.zeros((group_rows, weight.shape[1]), jnp.float32)
        piece_rows = lax.all_gather(queries, "label", axis=0, tiled=True)
        piece_pos = lax.all_gather(positives, "label", axis=0, tiled=True)
        resid = residuals(piece_rows, piece_pos, wb, label_ids)
        grad_acc = grad_acc + contract_first(resid, piece_rows)
        terms = jnp.dot(resid, wb, preferred_element_type=jnp.float32)
        rows_acc = lax.dynamic_update_slice_in_dim(rows_acc, terms, jnp.int32(0), 0)
        grad = grad_acc
        results.append(lax.psum_scatter(rows_acc, "label", scatter_dimension=0, tiled=True))
        grad = lax.psum(grad, "dp")
        weight, first, second = adamw(weight, first, second, grad, past_steps + step + 1)
    return (weight, first, second, jnp.stack(results))


def solution(mesh):
    in_specs = (
        P(("label", "dp"), None),
        P(("label", "dp"), None),
        P("label", None),
        P("label", None),
        P("label", None),
    )
    out_specs = (
        P("label", None),
        P("label", None),
        P("label", None),
        P(None, ("label", "dp"), None),
    )
    return jax.shard_map(shards, mesh=mesh, in_specs=in_specs, out_specs=out_specs, check_vma=False)
```

profile of v0, /device:TPU:1, one launch (start us, length us, event | category | flops | bytes accessed | tf_op | source)
XLA Modules:
  0.0 1541.0 jit_solution(326594451853943672)
XLA Ops:
  7.2 0.0 all-gather.3.cloned.1.call-start
  7.2 0.7 all-gather.3.cloned.1.call-update
  7.9 0.0 all-reduce.3.cloned.1.call-start
  7.9 162.8 %all-gather = s32[128,16,8]{1,2,0:T(8,128)S(1)} all-gather(s32[1,16,8]{1,2,0:T(8,128)} %bitcast.17), channel_id=1, replica_groups=mesh['label'=128,'dp'=2] {'label'}, dimensions={0}, use_global_device_ids=true | all-gather | bytes 66048 | tf_op jit(solution)/shard_map/all_gather | solution.py:57
  170.8 0.4 copy.20
  171.1 23.1 %compare_reduce_fusion = pred[2048,1024]{1,0:T(8,128)(4,1)} fusion(s32[1024]{0:T(1024)S(1)} %iota_add_fusion, s32[2048,8]{1,0:T(8,128)S(1)} %bitcast.14), kind=kLoop, calls=%fused_computation | loop fusion | flops 31457280 | bytes 2166784 | tf_op jit(solution)/shard_map/reduce_or | solution.py:31
  194.3 31.7 %all-gather.3.cloned.1.call-done = bf16[2048,512]{1,0:T(8,128)(2,1)} async-done(((bf16[16,512]{1,0:T(8,128)(2,1)}), bf16[2048,512]{1,0:T(8,128)(2,1)}) %all-gather.3.cloned.1.call-update) | async-done | bytes 2097168 | tf_op jit(solution)/shard_map/all_gather | solution.py:56
  226.0 6.5 fusion
  232.5 0.0 copy-start.4
  232.5 1.9 copy-done.4
  234.4 0.0 copy-done.1
  234.4 3.7 fusion.11
  238.1 0.0 all-reduce.3.cloned.1.call-update
  238.2 0.2 all-reduce.5.cloned.1.call-start
  238.4 76.1 %all-reduce.3.cloned.1.call-done = f32[1024,512]{1,0:T(8,128)} async-done(((f32[1024,512]{1,0:T(8,128)}), f32[1024,512]{1,0:T(8,128)}) %all-reduce.3.cloned.1.call-update) | async-done | bytes 2097168 | tf_op jit(solution)/shard_map/psum | solution.py:64
  314.5 4.4 multiply_subtract_fusion.1
  319.0 0.0 copy-start.3
  319.0 3.5 fusion.1
  322.5 2.0 copy-done.5
  324.4 3.7 fusion.12
  328.1 0.0 all-reduce.5.cloned.1.call-update
  328.1 0.0 reduce-scatter.3.cloned.1.call-start
  328.2 7.2 fusion.7
  335.3 0.0 reduce-scatter.3.cloned.1.call-update
  335.4 0.0 reduce-scatter.5.cloned.1.call-start
  335.4 7.2 fusion.4
  342.6 0.0 reduce-scatter.5.cloned.1.call-update
  342.6 61.2 %all-reduce.5.cloned.1.call-done = f32[1024,512]{1,0:T(8,128)} async-done(((f32[1024,512]{1,0:T(8,128)}), f32[1024,512]{1,0:T(8,128)}) %all-reduce.5.cloned.1.call-update) | async-done | bytes 2097168 | tf_op jit(solution)/shard_map/psum | solution.py:64
  403.9 7.6 multiply_subtract_fusion
  411.5 557.0 %reduce-scatter.3.cloned.1.call-done = f32[16,512]{1,0:T(8,128)} async-done(((f32[2048,512]{1,0:T(8,128)}), f32[16,512]{1,0:T(8,128)}) %reduce-scatter.3.cloned.1.call-update) | async-done | bytes 32784 | tf_op jit(solution)/shard_map/reduce_scatter | solution.py:63
  968.5 564.6 %reduce-scatter.5.cloned.1.call-done = f32[16,512]{1,0:T(8,128)} async-done(((f32[2048,512]{1,0:T(8,128)}), f32[16,512]{1,0:T(8,128)}) %reduce-scatter.5.cloned.1.call-update) | async-done | bytes 32784 | tf_op jit(solution)/shard_map/reduce_scatter | solution.py:63
  1533.0 1.4 pad_maximum_fusion
  (10 shorter events, 0.0 us)
Async XLA Ops:
  7.2 218.8 %all-gather.3.cloned.1.call-start = ((), (), s32[]{:S(2)}) async-start(), calls=%async_computation.2 | async-start | bytes 2113536 | tf_op jit(solution)/shard_map/all_gather | solution.py:56
  7.9 306.6 %all-reduce.3.cloned.1.call-start = ((), (), s32[]{:S(2)}) async-start(), calls=%async_computation.3 | async-start | bytes 4194304 | tf_op jit(solution)/shard_map/psum | solution.py:64
  226.0 8.4 copy-start.1
  232.5 2.0 copy-start.4
  238.1 76.4 %copy-start = (f32[1024,512]{1,0:T(8,128)S(1)}, f32[1024,512]{1,0:T(8,128)}, u32[]{:S(2)}) copy-start(f32[1024,512]{1,0:T(8,128)} %param.8) | copy-start | bytes 6291460
  238.2 165.7 %all-reduce.5.cloned.1.call-start = ((), (), s32[]{:S(2)}) async-start(), calls=%async_computation.4 | async-start | bytes 4194304 | tf_op jit(solution)/shard_map/psum | solution.py:64
  314.5 4.4 copy-start.2
  314.5 4.5 copy-start.6
  319.0 3.5 copy-start.3
  322.5 2.0 copy-start.5
  328.1 640.3 %reduce-scatter.3.cloned.1.call-start = ((), (), s32[]{:S(2)}) async-start(), calls=%async_computation.5 | async-start | bytes 4227072 | tf_op jit(solution)/shard_map/reduce_scatter | solution.py:63
  335.4 1197.7 %reduce-scatter.5.cloned.1.call-start = ((), (), s32[]{:S(2)}) async-start(), calls=%async_computation.6 | async-start | bytes 4227072 | tf_op jit(solution)/shard_map/reduce_scatter | solution.py:63
Sparse Core Ops, SparseCore 0:
  9.9 216.0 all-gather.2
  238.3 76.1 all-reduce.2
  328.3 75.5 all-reduce.4
  406.2 562.1 reduce-scatter.2
  971.0 562.0 reduce-scatter.4
where the time goes:
time: 1550 us; the launch traced here: 1540 us
  waiting for transfers between devices  1290 us (83%)
  blocking collectives  163 us (11%)
  other arithmetic  36.6 us (2%)
  matrix products  31.6 us (2%)
    reduce_scatter x2, waiting for transfers between devices, shards(): lax.psum_scatter(rows_acc, 'label', scatter_dimension=0, tiled=True)  1120 us
    all_gather x1, blocking collectives, shards(): piece_pos = lax.all_gather(positives, 'label', axis=0, tiled=True)  163 us
    psum x2, waiting for transfers between devices, shards(): grad = lax.psum(grad, 'dp')  137 us
    all_gather x1, waiting for transfers between devices, shards(): piece_rows = lax.all_gather(queries, 'label', axis=0, tiled=True)  31.7 us
  transfers between devices with their start and end apart: 5, of which 5 were waited for; matrix products, arithmetic and copies ran while one was open for 3% of the time, Pallas kernels for 0%

commit v1 on v0

v1 whole, which is shorter than its diff:
```python
import jax
import jax.numpy as jnp
from jax import lax
from jax.experimental import pallas as pl
from jax.experimental.pallas import tpu as pltpu
from jax.sharding import Mesh, PartitionSpec as P

STEPS = 2

beta_one = 0.9
beta_two = 0.95
rate = 0.02
decay = 0.1
epsilon = 1e-08
past_steps = 1000

f32 = jnp.float32
bf16 = jnp.bfloat16
i32 = jnp.int32

NX, NLO, NZ, NCORE, NHI = 4, 2, 8, 2, 2
NY = NLO * NHI
D = 512
ROWS = 16
LINE = NZ * ROWS
HALF = LINE // 2
PAD = 80
NQ = NX * NY * LINE
BLOCK = 256
NBLOCK = NQ // BLOCK
LAB = 1024
TILE = 256
SLOTS = 8
VMEM = 40 * 2**20


def spec(shape=None, index=None, space=pltpu.VMEM):
    if shape is None:
        return pl.BlockSpec(memory_space=space)
    return pl.BlockSpec(shape, index, memory_space=space)


SMEM = pltpu.SMEM


def params():
    return pltpu.CompilerParams(vmem_limit_bytes=VMEM)


def descending(rows):
    rows = list(rows)
    for a, b in (
        (0, 1), (2, 3), (4, 5), (6, 7), (0, 2), (1, 3), (4, 6), (5, 7), (1, 2), (5, 6),
        (0, 4), (1, 5), (2, 6), (3, 7), (2, 4), (3, 5), (1, 2), (3, 4), (5, 6),
    ):
        rows[a], rows[b] = jnp.maximum(rows[a], rows[b]), jnp.minimum(rows[a], rows[b])
    return rows


def assemble_kernel(meta, *refs):
    left, right, (q_ref, pos_ref, most_ref) = refs[:4], refs[4:8], refs[8:]
    base = meta[1]

    def fill(shift):
        for c in range(NY):
            dy = (c + shift) % NY
            most = []
            for dx in range(NX):
                at = c * NX * LINE + dx * LINE
                q_ref[at : at + HALF, :] = left[dy][dx, :HALF, :]
                q_ref[at + HALF : at + LINE, :] = right[dx][dy]
                coded = left[dy][dx, HALF:PAD, : 3 * LINE].astype(f32)[:SLOTS]
                ids = coded[:, :LINE] + 256.0 * coded[:, LINE : 2 * LINE] + 65536.0 * coded[:, 2 * LINE :]
                local = ids.astype(i32) - base
                local = jnp.where((local >= 0) & (local < NCORE * LAB), local, -1)
                rows = descending([local[j : j + 1, :] for j in range(SLOTS)])
                for j in range(SLOTS):
                    pos_ref[j : j + 1, at : at + LINE] = rows[j]
                most.append(sum((row >= 0).astype(f32) for row in rows))
            for pair in range(2):
                both = jnp.maximum(most[2 * pair], most[2 * pair + 1])
                most_ref[2 * c + pair] = jnp.max(both).astype(i32)

    pl.when(meta[0] == 0)(lambda: fill(0))
    pl.when(meta[0] == 1)(lambda: fill(NLO))


def assemble(meta, left, right):
    return pl.pallas_call(
        assemble_kernel,
        out_shape=(
            jax.ShapeDtypeStruct((NQ, D), bf16),
            jax.ShapeDtypeStruct((SLOTS, NQ), i32),
            jax.ShapeDtypeStruct((NBLOCK,), i32),
        ),
        in_specs=[spec(space=SMEM)] + [spec()] * 8,
        out_specs=(spec(), spec(), spec(space=SMEM)),
        compiler_params=params(),
        cost_estimate=pl.CostEstimate(flops=0, bytes_accessed=4 * NQ * D, transcendentals=0),
        name="assemble",
    )(meta, *left, *right)


def resid_kernel(offset, most, q_ref, pos_ref, wb_ref, out_ref):
    count = most[pl.program_id(0)]

    def fill(slots):
        q = q_ref[...]
        for t in range(LAB // TILE):
            rows = slice(t * TILE, (t + 1) * TILE)
            logits = lax.dot_general(
                wb_ref[rows, :], q, (((1,), (1,)), ((), ())), preferred_element_type=f32
            )
            share = pl.reciprocal(1.0 + jnp.exp(-logits), approx=True)
            label = lax.broadcasted_iota(i32, (TILE, BLOCK), 0)
            start = offset[0] + t * TILE
            hit = (pos_ref[0:1, :] - start) == label
            for j in range(1, slots):
                hit = hit | ((pos_ref[j : j + 1, :] - start) == label)
            out_ref[rows, :] = jnp.where(hit, share - 1.0, share).astype(bf16)

    pl.when(count <= 1)(lambda: fill(1))
    pl.when(count == 2)(lambda: fill(2))
    pl.when(count > 2)(lambda: fill(SLOTS))


def residuals(offset, most, q, pos, wb):
    return pl.pallas_call(
        resid_kernel,
        grid=(NBLOCK,),
        out_shape=jax.ShapeDtypeStruct((LAB, NQ), bf16),
        in_specs=[
            spec(space=SMEM),
            spec(space=SMEM),
            spec((BLOCK, D), lambda i: (i, 0)),
            spec((SLOTS, BLOCK), lambda i: (0, i)),
            spec((LAB, D), lambda i: (0, 0)),
        ],
        out_specs=spec((LAB, BLOCK), lambda i: (0, i)),
        compiler_params=params(),
        cost_estimate=pl.CostEstimate(
            flops=2 * LAB * NQ * D, bytes_accessed=2 * (NQ * D + LAB * D + LAB * NQ), transcendentals=2 * LAB * NQ
        ),
        name="resid",
    )(offset, most, q, pos, wb)


def terms_kernel(blocks, own_ref, other_ref, wb_own, wb_other, out_ref):
    dims = (((0,), (0,)), ((), ()))
    out_ref[...] = lax.dot_general(own_ref[...], wb_own[...], dims, preferred_element_type=f32) + lax.dot_general(
        other_ref[...], wb_other[...], dims, preferred_element_type=f32
    )


def terms(blocks, first, second, wb_first, wb_second):
    count = blocks.shape[0]
    return pl.pallas_call(
        terms_kernel,
        grid_spec=pltpu.PrefetchScalarGridSpec(
            num_scalar_prefetch=1,
            grid=(count,),
            in_specs=[
                spec((LAB, BLOCK), lambda i, blocks: (0, blocks[i])),
                spec((LAB, BLOCK), lambda i, blocks: (0, blocks[i])),
                spec((LAB, D), lambda i, blocks: (0, 0)),
                spec((LAB, D), lambda i, blocks: (0, 0)),
            ],
            out_specs=spec((BLOCK, D), lambda i, blocks: (i, 0)),
        ),
        out_shape=jax.ShapeDtypeStruct((count * BLOCK, D), f32),
        compiler_params=params(),
        cost_estimate=pl.CostEstimate(
            flops=4 * LAB * count * BLOCK * D, bytes_accessed=8 * 2**20, transcendentals=0
        ),
        name="terms",
    )(blocks, first, second, wb_first, wb_second)


def grad_kernel(resid_ref, q_ref, out_ref):
    out_ref[...] = jnp.dot(resid_ref[...], q_ref[...], preferred_element_type=f32)


def gradient(resid, q):
    return pl.pallas_call(
        grad_kernel,
        grid=(LAB // TILE,),
        out_shape=jax.ShapeDtypeStruct((LAB, D), f32),
        in_specs=[spec((TILE, NQ), lambda i: (i, 0)), spec((NQ, D), lambda i: (0, 0))],
        out_specs=spec((TILE, D), lambda i: (i, 0)),
        compiler_params=params(),
        cost_estimate=pl.CostEstimate(
            flops=2 * LAB * NQ * D, bytes_accessed=2 * (LAB * NQ + NQ * D) + 4 * LAB * D, transcendentals=0
        ),
        name="grad",
    )(resid, q)


def adamw_kernel(count, resid_ref, q_ref, part_ref, w_ref, m_ref, v_ref, w_out, m_out, v_out, *wb_out):
    grad = jnp.dot(resid_ref[...], q_ref[...], preferred_element_type=f32) + part_ref[...]
    first = beta_one * m_ref[...] + (1.0 - beta_one) * grad
    second = beta_two * v_ref[...] + (1.0 - beta_two) * grad * grad
    first_hat = first / (1.0 - beta_one**count)
    second_hat = second / (1.0 - beta_two**count)
    weight = w_ref[...]
    weight = weight - rate * (first_hat / (jnp.sqrt(second_hat) + epsilon) + decay * weight)
    w_out[...] = weight
    m_out[...] = first
    v_out[...] = second
    if wb_out:
        wb_out[0][...] = weight.astype(bf16)


def update(count, last, resid, q, part, weight, first, second):
    tile = spec((TILE, D), lambda i: (i, 0))
    full = jax.ShapeDtypeStruct((LAB, D), f32)
    return pl.pallas_call(
        lambda *refs: adamw_kernel(count, *refs),
        grid=(LAB // TILE,),
        out_shape=(full, full, full) + (() if last else (jax.ShapeDtypeStruct((LAB, D), bf16),)),
        in_specs=[spec((TILE, NQ), lambda i: (i, 0)), spec((NQ, D), lambda i: (0, 0))] + [tile] * 4,
        out_specs=(tile,) * (3 if last else 4),
        compiler_params=params(),
        cost_estimate=pl.CostEstimate(
            flops=2 * LAB * NQ * D, bytes_accessed=2 * (LAB * NQ + NQ * D) + 28 * LAB * D, transcendentals=2 * LAB * D
        ),
        name="adamw",
    )(resid, q, part, weight, first, second)


def shift(array, axis, by):
    if axis == "x":
        return lax.ppermute(array, "x", [(i, (i + by) % NX) for i in range(NX)])
    name = lambda y: (y % NLO) * NHI + y // NLO
    return lax.ppermute(array, ("ylo", "yhi"), [(name(y), name((y + by) % NY)) for y in range(NY)])


def swap(array):
    return lax.ppermute(array, "core", [(0, 1), (1, 0)])


def spread(array, axis):
    near = shift(array, axis, -1)
    far = shift(array, axis, 1)
    mid = shift(array, axis, 2)
    return [array, near, mid, far]


def gather(queries, positives):
    coded = positives.T.reshape(1, ROWS * SLOTS)
    pieces = [coded & 255, (coded >> 8) & 255, coded >> 16]
    pieces.append(jnp.zeros_like(coded))
    coded = jnp.concatenate(pieces, axis=1).astype(bf16)
    mine = jnp.concatenate([queries, coded, jnp.zeros((7, D), bf16)], axis=0)
    line = lax.all_to_all(
        jnp.broadcast_to(mine[None], (NZ, ROWS + 8, D)), "z", split_axis=0, concat_axis=0, tiled=True
    )
    rows = line[:, :ROWS].reshape(LINE, D)
    coded = line[:, ROWS, : 3 * LINE].reshape(NZ, 3, SLOTS, ROWS)
    coded = coded.transpose(2, 1, 0, 3).reshape(SLOTS, 3 * LINE)
    coded = jnp.pad(coded, ((0, PAD - HALF - SLOTS), (0, D - 3 * LINE)))
    left = jnp.concatenate([rows[:HALF], coded], axis=0)
    right = rows[HALF:]
    left = jnp.stack(spread(left, "x"))
    right = jnp.stack(spread(right, "y"))
    return spread(left, "y"), spread(right, "x")


def scatter_plane(parts):
    up = shift(parts[:BLOCK].astype(bf16), "y", 1)
    down = shift(parts[BLOCK : 2 * BLOCK].astype(bf16), "y", -1)
    plane = parts[2 * BLOCK :] + jnp.concatenate([up, down], axis=0).astype(f32)
    plane = plane.reshape(NX, LINE, D)
    got = [shift(plane[dx].astype(bf16), "x", dx) for dx in (1, 3, 2)]
    line = plane[0] + got[0].astype(f32) + got[1].astype(f32) + got[2].astype(f32)
    return line.reshape(NZ, ROWS, D)


def shards(queries, positives, weights, first_moment, second_moment):
    weight, first, second = weights, first_moment, second_moment
    core, high = lax.axis_index("core"), lax.axis_index("yhi")
    chip = (lax.axis_index("x") * NLO + lax.axis_index("ylo")) * NZ + lax.axis_index("z")
    meta = jnp.stack([high, chip * (NCORE * LAB)]).astype(i32)
    mine = (core * LAB).astype(i32).reshape(1)
    theirs = ((1 - core) * LAB).astype(i32).reshape(1)
    here = 4 * high
    blocks = jnp.stack([here + 2, 7 - here, here, here + 1]).astype(i32)

    wb = weight.astype(bf16)
    wb_other = swap(wb)
    left, right = gather(queries, positives)
    q, pos, most = assemble(meta, left, right)
    lines = []
    for step in range(STEPS):
        own = residuals(mine, most, q, pos, wb)
        other = residuals(theirs, most, q, pos, wb_other)
        parts = terms(blocks, own, other, wb, wb_other)
        part = swap(gradient(other, q))
        last = step == STEPS - 1
        out = update(past_steps + step + 1, last, own, q, part, weight, first, second)
        weight, first, second = out[:3]
        lines.append(scatter_plane(parts))
        if not last:
            wb = out[3]
            wb_other = swap(wb)
    line = jnp.stack(lines, axis=1)
    line = lax.all_to_all(line, "z", split_axis=0, concat_axis=0, tiled=True)
    return weight, first, second, jnp.sum(line, axis=0)


def solution(mesh):
    axes = ("x", "ylo", "z", "core", "yhi")
    devices = mesh.devices.reshape(NX, NLO, NZ, NCORE, NHI)
    label = ("x", "ylo", "z", "core")
    in_specs = (P(axes, None), P(axes, None), P(label, None), P(label, None), P(label, None))
    out_specs = (P(label, None), P(label, None), P(label, None), P(None, axes, None))
    return jax.shard_map(
        shards, mesh=Mesh(devices, axes), in_specs=in_specs, out_specs=out_specs, check_vma=False
    )
```

time: 1550 us -> 192 us (0.12)
  the two profiles are of different devices: /device:TPU:1 before, /device:TPU:6 now
where the time goes in v1:
time: 192 us; the launch traced here: 190 us
  Pallas kernels  59.4 us (31%)
  starting transfers between devices  46.4 us (24%)
  waiting for transfers between devices  31.7 us (17%)
  local copies, waits for them, and re-layouts  24.3 us (13%)
  blocking collectives  22.1 us (12%)
  other arithmetic  4.93 us (3%)
    pallas_call x4, Pallas kernels, residuals(): pl.pallas_call(resid_kernel, grid=(NBLOCK,), out_shape=jax.ShapeDtypeStru...  25.9 us
    ppermute x12, starting transfers between devices, shift(): return lax.ppermute(array, 'x', [(i, (i + by) % NX) for i in range(NX)])  23 us
    unnamed x56, local copies, waits for them, and re-layouts  22.9 us
    all_to_all x1, blocking collectives, shards(): line = lax.all_to_all(line, 'z', split_axis=0, concat_axis=0, tiled=True)  22.1 us
    pallas_call x2, Pallas kernels, update(): pl.pallas_call(lambda *refs: adamw_kernel(count, *refs), grid=(LAB // TIL...  14.5 us
    ppermute x10, starting transfers between devices, shift(): lax.ppermute(array, ('ylo', 'yhi'), [(name(y), name((y + by) % NY)) for y...  14.5 us
    ppermute x12, waiting for transfers between devices, shift(): return lax.ppermute(array, 'x', [(i, (i + by) % NX) for i in range(NX)])  13.2 us
    ppermute x10, waiting for transfers between devices, shift(): lax.ppermute(array, ('ylo', 'yhi'), [(name(y), name((y + by) % NY)) for y...  9.8 us
  transfers between devices with their start and end apart: 27, of which 8 were waited for; matrix products, arithmetic and copies ran while one was open for 2% of the time, Pallas kernels for 12%

profile of v1, /device:TPU:6, one launch (start us, length us, event | category | flops | bytes accessed | tf_op | source)
XLA Modules:
  0.0 189.8 jit_solution(16596447996417547791)
XLA Ops:
  3.2 8.5 %all-to-all-start = ((bf16[8,24,512]{2,1,0:T(8,128)(2,1)}), bf16[8,24,512]{2,1,0:T(8,128)(2,1)S(1)}, u32[]{:S(2)}, u32[]{:S(2)}) async-start(bf16[8,24,512]{2,1,0:T(8,128)(2,1)} %broadcast_in_dim.14), calls=%async_computation | async-start | bytes 393216 | tf_op jit(solution)/shard_map/all_to_all | solution.py:254
  11.6 1.7 convert_element_type.48.wb_ref.wb_own
  13.5 8.6 %all-to-all-done = bf16[8,24,512]{2,1,0:T(8,128)(2,1)S(1)} async-done(((bf16[8,24,512]{2,1,0:T(8,128)(2,1)}), bf16[8,24,512]{2,1,0:T(8,128)(2,1)S(1)}, u32[]{:S(2)}, u32[]{:S(2)}) %all-to-all-start) | async-done | bytes 196640 | tf_op jit(solution)/shard_map/all_to_all | solution.py:254
  22.1 3.1 %collective-permute-start.6 = (bf16[64,512]{1,0:T(8,128)(2,1)S(1)}, bf16[64,512]{1,0:T(8,128)(2,1)S(1)}, u32[]{:S(2)}, u32[]{:S(2)}) collective-permute-start(bf16[64,512]{1,0:T(8,128)(2,1)S(1)} %bitcast.37), channel_id=1, source_target_pairs={{0,33},{32,0},{1,32},{33,1},{2,35},{34,2},{3,34},{35,3},{4,37},{36... | collective-permute-start | bytes 196616 | tf_op jit(solution)/shard_map/ppermute | solution.py:234
  28.6 2.4 %collective-permute-done.7 = bf16[64,512]{1,0:T(8,128)(2,1)S(1)} collective-permute-done((bf16[64,512]{1,0:T(8,128)(2,1)S(1)}, bf16[64,512]{1,0:T(8,128)(2,1)S(1)}, u32[]{:S(2)}, u32[]{:S(2)}) %collective-permute-start.7) | collective-permute-done | bytes 65568 | tf_op jit(solution)/shard_map/ppermute | solution.py:234
  33.2 2.1 %collective-permute-start.2 = (bf16[80,512]{1,0:T(8,128)(2,1)S(1)}, bf16[80,512]{1,0:T(8,128)(2,1)S(1)}, u32[]{:S(2)}, u32[]{:S(2)}) collective-permute-start(bf16[80,512]{1,0:T(8,128)(2,1)S(1)} %get-tuple-element.41), channel_id=1, source_target_pairs={{0,64},{64,128},{128,192},{192,0},{1,65},{65,129},{129,193},{193,1... | collective-permute-start | bytes 245768 | tf_op jit(solution)/shard_map/ppermute | solution.py:232
  35.3 3.2 %collective-permute-start.11 = (bf16[4,64,512]{2,1,0:T(8,128)(2,1)S(1)}, bf16[4,64,512]{2,1,0:T(8,128)(2,1)S(1)}, u32[]{:S(2)}, u32[]{:S(2)}) collective-permute-start(bf16[4,64,512]{2,1,0:T(8,128)(2,1)S(1)} %pad_maximum_fusion.2.refs_4_), channel_id=1, source_target_pairs={{0,64},{64,128},{128,192},{192,0},{1,65},{65,129},{129,193},{193,1... | collective-permute-start | bytes 786440 | tf_op jit(solution)/shard_map/ppermute | solution.py:232
  38.6 2.6 %collective-permute-done.2 = bf16[80,512]{1,0:T(8,128)(2,1)S(1)} collective-permute-done((bf16[80,512]{1,0:T(8,128)(2,1)S(1)}, bf16[80,512]{1,0:T(8,128)(2,1)S(1)}, u32[]{:S(2)}, u32[]{:S(2)}) %collective-permute-start.2) | collective-permute-done | bytes 81952 | tf_op jit(solution)/shard_map/ppermute | solution.py:232
  47.0 6.3 %collective-permute-done.9.refs_5_ = bf16[4,64,512]{2,1,0:T(8,128)(2,1)S(1)} collective-permute-done((bf16[4,64,512]{2,1,0:T(8,128)(2,1)S(1)}, bf16[4,64,512]{2,1,0:T(8,128)(2,1)S(1)}, u32[]{:S(2)}, u32[]{:S(2)}) %collective-permute-start.9) | collective-permute-done | bytes 262176 | tf_op jit(solution)/shard_map/ppermute | solution.py:232
  64.6 7.0 %resid.5.resid_ref.other_ref = bf16[1024,2048]{1,0:T(8,128)(2,1)S(1)} custom-call(s32[1]{0:T(128)} %bitcast.17.offset, s32[8]{0:T(128)S(1)} %get-tuple-element.14.most, bf16[2048,512]{1,0:T(8,128)(2,1)S(1)} %get-tuple-element.15.q_ref.refs_1_, s32[8,2048]{1,0:T(8,128)S(1)} %get-tuple-element.16.pos_ref, bf16[1024,512]{1,0:T(8,128)(2,1)} %collective-permute-done.12.wb_ref.wb_other), custom_call_target="tpu_custom_call" | custom-call | flops 2147483648 | bytes 7340032 | tf_op jit(solution)/shard_map/resid/pallas_call | solution.py:128
  71.6 4.2 %grad.2 = f32[1024,512]{1,0:T(8,128)} custom-call(bf16[1024,2048]{1,0:T(8,128)(2,1)S(1)} %resid.5.resid_ref.other_ref, bf16[2048,512]{1,0:T(8,128)(2,1)S(1)} %get-tuple-element.15.q_ref.refs_1_), custom_call_target="tpu_custom_call" | custom-call | flops 2147483648 | bytes 8388608 | tf_op jit(solution)/shard_map/grad/pallas_call | solution.py:184
  75.9 6.3 %resid.4.refs_0_.own_ref = bf16[1024,2048]{1,0:T(8,128)(2,1)S(1)} custom-call(s32[1]{0:T(128)} %bitcast.offset, s32[8]{0:T(128)S(1)} %get-tuple-element.14.most, bf16[2048,512]{1,0:T(8,128)(2,1)S(1)} %get-tuple-element.15.q_ref.refs_1_, s32[8,2048]{1,0:T(8,128)S(1)} %get-tuple-element.16.pos_ref, bf16[1024,512]{1,0:T(8,128)(2,1)S(1)} %convert_element_type.48.wb_ref.wb_own), custom_call_target="tpu_custom_call" | custom-call | flops 2147483648 | bytes 7340032 | tf_op jit(solution)/shard_map/resid/pallas_call | solution.py:128
  82.2 2.0 %copy-done.1 = bf16[1024,2048]{1,0:T(8,128)(2,1)} copy-done((bf16[1024,2048]{1,0:T(8,128)(2,1)}, bf16[1024,2048]{1,0:T(8,128)(2,1)S(1)}, u32[]{:S(2)}) %copy-start.1) | copy-done | bytes 4194328
  84.2 6.9 %adamw.2 = (f32[1024,512]{1,0:T(8,128)S(1)}, f32[1024,512]{1,0:T(8,128)S(1)}, f32[1024,512]{1,0:T(8,128)S(1)}, bf16[1024,512]{1,0:T(8,128)(2,1)S(1)}) custom-call(bf16[1024,2048]{1,0:T(8,128)(2,1)} %copy-done.1, bf16[2048,512]{1,0:T(8,128)(2,1)S(1)} %get-tuple-element.15.q_ref.refs_1_, f32[1024,512]{1,0:T(8,128)} %collective-permute-done.13.refs_2_, ...), custom_call_target="tpu_custom_call" | custom-call | flops 2147483648 | bytes 20971520 | tf_op jit(solution)/shard_map/adamw/pallas_call | solution.py:216
  92.8 3.7 %copy-done.4 = bf16[1024,2048]{1,0:T(8,128)(2,1)S(1)} copy-done((bf16[1024,2048]{1,0:T(8,128)(2,1)S(1)}, bf16[1024,2048]{1,0:T(8,128)(2,1)}, u32[]{:S(2)}) %copy-start.4) | copy-done | bytes 4194328
  96.5 5.2 %terms.2 = f32[1024,512]{1,0:T(8,128)S(1)} custom-call(s32[4]{0:T(128)S(1)} %pad_add_fusion.1.blocks, bf16[1024,2048]{1,0:T(8,128)(2,1)S(1)} %copy-done.2, bf16[1024,2048]{1,0:T(8,128)(2,1)S(1)} %copy-done.4, bf16[1024,512]{1,0:T(8,128)(2,1)S(1)} %convert_element_type.48.wb_ref.wb_own, bf16[1024,512]{1,0:T(8,128)(2,1)} %collective-permute-done.12.wb_ref.wb_other), custom_call_target="tpu_custom_call" | custom-call | flops 2147483648 | bytes 8388608 | tf_op jit(solution)/shard_map/terms/pallas_call | solution.py:157
  103.6 1.8 collective-permute-start.17
  105.4 6.7 %collective-permute-done.16 = bf16[256,512]{1,0:T(8,128)(2,1)S(1)} collective-permute-done((bf16[256,512]{1,0:T(8,128)(2,1)S(1)}, bf16[256,512]{1,0:T(8,128)(2,1)S(1)}, u32[]{:S(2)}, u32[]{:S(2)}) %collective-permute-start.16) | collective-permute-done | bytes 262176 | tf_op jit(solution)/shard_map/ppermute | solution.py:234
  112.3 6.3 %resid.6.refs_0_.own_ref = bf16[1024,2048]{1,0:T(8,128)(2,1)S(1)} custom-call(s32[1]{0:T(128)} %bitcast.offset, s32[8]{0:T(128)S(1)} %get-tuple-element.14.most, bf16[2048,512]{1,0:T(8,128)(2,1)S(1)} %get-tuple-element.15.q_ref.refs_1_, s32[8,2048]{1,0:T(8,128)S(1)} %get-tuple-element.16.pos_ref, bf16[1024,512]{1,0:T(8,128)(2,1)S(1)} %get-tuple-element.17.wb_ref.wb_own), custom_call_target="tpu_custom_call" | custom-call | flops 2147483648 | bytes 7340032 | tf_op jit(solution)/shard_map/resid/pallas_call | solution.py:128
  118.6 6.3 %resid.7.resid_ref.other_ref = bf16[1024,2048]{1,0:T(8,128)(2,1)S(1)} custom-call(s32[1]{0:T(128)} %bitcast.17.offset, s32[8]{0:T(128)S(1)} %get-tuple-element.14.most, bf16[2048,512]{1,0:T(8,128)(2,1)S(1)} %get-tuple-element.15.q_ref.refs_1_, s32[8,2048]{1,0:T(8,128)S(1)} %get-tuple-element.16.pos_ref, ...), custom_call_target="tpu_custom_call" | custom-call | flops 2147483648 | bytes 7340032 | tf_op jit(solution)/shard_map/resid/pallas_call | solution.py:128
  125.0 4.2 %terms.3 = f32[1024,512]{1,0:T(8,128)S(1)} custom-call(s32[4]{0:T(128)S(1)} %pad_add_fusion.1.blocks, bf16[1024,2048]{1,0:T(8,128)(2,1)S(1)} %resid.6.refs_0_.own_ref, bf16[1024,2048]{1,0:T(8,128)(2,1)S(1)} %resid.7.resid_ref.other_ref, bf16[1024,512]{1,0:T(8,128)(2,1)S(1)} %copy-done.13, bf16[1024,512]{1,0:T(8,128)(2,1)S(1)} %collective-permute-done.14.wb_ref.wb_other), custom_call_target="tpu_custom_call" | custom-call | flops 2147483648 | bytes 8388608 | tf_op jit(solution)/shard_map/terms/pallas_call | solution.py:157
  130.6 2.1 %collective-permute-start.22 = (bf16[256,512]{1,0:T(8,128)(2,1)S(1)}, bf16[256,512]{1,0:T(8,128)(2,1)S(1)}, u32[]{:S(2)}, u32[]{:S(2)}) collective-permute-start(bf16[256,512]{1,0:T(8,128)(2,1)S(1)} %get-tuple-element.31), channel_id=1, source_target_pairs={{0,33},{32,0},{1,32},{33,1},{2,35},{34,2},{3,34},{35,3},{4,37},{36... | collective-permute-start | bytes 786440 | tf_op jit(solution)/shard_map/ppermute | solution.py:234
  132.6 3.7 %grad.3 = f32[1024,512]{1,0:T(8,128)} custom-call(bf16[1024,2048]{1,0:T(8,128)(2,1)S(1)} %resid.7.resid_ref.other_ref, bf16[2048,512]{1,0:T(8,128)(2,1)S(1)} %get-tuple-element.15.q_ref.refs_1_), custom_call_target="tpu_custom_call" | custom-call | flops 2147483648 | bytes 8388608 | tf_op jit(solution)/shard_map/grad/pallas_call | solution.py:184
  136.4 1.7 collective-permute-start.18
  138.1 1.7 collective-permute-start.19
  139.9 2.0 %collective-permute-start.20 = (bf16[128,512]{1,0:T(8,128)(2,1)S(1)}, bf16[128,512]{1,0:T(8,128)(2,1)S(1)}, u32[]{:S(2)}, u32[]{:S(2)}) collective-permute-start(bf16[128,512]{1,0:T(8,128)(2,1)S(1)} %get-tuple-element.33), channel_id=1, source_target_pairs={{0,128},{64,192},{128,0},{192,64},{1,129},{65,193},{129,1},{193,65... | collective-permute-start | bytes 393224 | tf_op jit(solution)/shard_map/ppermute | solution.py:232
  142.1 2.7 %collective-permute-start.23 = (bf16[128,512]{1,0:T(8,128)(2,1)S(1)}, bf16[128,512]{1,0:T(8,128)(2,1)S(1)}, u32[]{:S(2)}, u32[]{:S(2)}) collective-permute-start(bf16[128,512]{1,0:T(8,128)(2,1)S(1)} %get-tuple-element.35), channel_id=1, source_target_pairs={{0,64},{64,128},{128,192},{192,0},{1,65},{65,129},{129,193},{193,1... | collective-permute-start | bytes 393224 | tf_op jit(solution)/shard_map/ppermute | solution.py:232
  144.8 3.3 %collective-permute-start.24 = (bf16[128,512]{1,0:T(8,128)(2,1)S(1)}, bf16[128,512]{1,0:T(8,128)(2,1)S(1)}, u32[]{:S(2)}, u32[]{:S(2)}) collective-permute-start(bf16[128,512]{1,0:T(8,128)(2,1)S(1)} %get-tuple-element.37), channel_id=1, source_target_pairs={{0,192},{64,0},{128,64},{192,128},{1,193},{65,1},{129,65},{193,129... | collective-permute-start | bytes 393224 | tf_op jit(solution)/shard_map/ppermute | solution.py:232
  148.1 2.0 %collective-permute-start.25 = (bf16[128,512]{1,0:T(8,128)(2,1)S(1)}, bf16[128,512]{1,0:T(8,128)(2,1)S(1)}, u32[]{:S(2)}, u32[]{:S(2)}) collective-permute-start(bf16[128,512]{1,0:T(8,128)(2,1)S(1)} %get-tuple-element.36), channel_id=1, source_target_pairs={{0,128},{64,192},{128,0},{192,64},{1,129},{65,193},{129,1},{193,65... | collective-permute-start | bytes 393224 | tf_op jit(solution)/shard_map/ppermute | solution.py:232
  151.7 2.8 %collective-permute-done.25 = bf16[128,512]{1,0:T(8,128)(2,1)S(1)} collective-permute-done((bf16[128,512]{1,0:T(8,128)(2,1)S(1)}, bf16[128,512]{1,0:T(8,128)(2,1)S(1)}, u32[]{:S(2)}, u32[]{:S(2)}) %collective-permute-start.25) | collective-permute-done | bytes 131104 | tf_op jit(solution)/shard_map/ppermute | solution.py:232
  154.7 22.1 %all_to_all.10 = f32[8,2,16,512]{3,2,1,0:T(8,128)S(1)} all-to-all(f32[8,2,16,512]{3,2,1,0:T(8,128)S(1)} %pad_maximum_fusion), channel_id=1, replica_groups=mesh['x'=4,'ylo'=2,'z'=8,'core'=2,'yhi'=2] {'z'}, dimensions={0} | all-to-all | bytes 1048576 | tf_op jit(solution)/shard_map/all_to_all | solution.py:306
  182.2 7.6 %adamw.3 = (f32[1024,512]{1,0:T(8,128)}, f32[1024,512]{1,0:T(8,128)}, f32[1024,512]{1,0:T(8,128)}) custom-call(bf16[1024,2048]{1,0:T(8,128)(2,1)} %copy-done, bf16[2048,512]{1,0:T(8,128)(2,1)S(1)} %get-tuple-element.15.q_ref.refs_1_, f32[1024,512]{1,0:T(8,128)} %collective-permute-done.15.refs_2_, f32[1024,512]{1,0:T(8,128)S(1)} %copy-done.7, ...), custom_call_target="tpu_custom_call" | custom-call | flops 2147483648 | bytes 20971520 | tf_op jit(solution)/shard_map/adamw/pallas_call | solution.py:216
  (122 shorter events, 38.0 us)
Async XLA Ops:
  3.2 18.9 %all-to-all-start = ((bf16[8,24,512]{2,1,0:T(8,128)(2,1)}), bf16[8,24,512]{2,1,0:T(8,128)(2,1)S(1)}, u32[]{:S(2)}, u32[]{:S(2)}) async-start(bf16[8,24,512]{2,1,0:T(8,128)(2,1)} %broadcast_in_dim.14), calls=%async_computation | async-start | bytes 393216 | tf_op jit(solution)/shard_map/all_to_all | solution.py:254
  13.4 51.2 %collective-permute-start.12 = (bf16[1024,512]{1,0:T(8,128)(2,1)S(1)}, bf16[1024,512]{1,0:T(8,128)(2,1)}, u32[]{:S(2)}, u32[]{:S(2)}) collective-permute-start(bf16[1024,512]{1,0:T(8,128)(2,1)S(1)} %convert_element_type.48.wb_ref.wb_own), channel_id=1, source_target_pairs={{0,2},{2,0},{1,3},{3,1},{4,6},{6,4},{5,7},{7,5},{8,10},{10,8},{9,1... | collective-permute-start | bytes 3145736 | tf_op jit(solution)/shard_map/ppermute | solution.py:238
  22.1 6.5 %collective-permute-start.6 = (bf16[64,512]{1,0:T(8,128)(2,1)S(1)}, bf16[64,512]{1,0:T(8,128)(2,1)S(1)}, u32[]{:S(2)}, u32[]{:S(2)}) collective-permute-start(bf16[64,512]{1,0:T(8,128)(2,1)S(1)} %bitcast.37), channel_id=1, source_target_pairs={{0,33},{32,0},{1,32},{33,1},{2,35},{34,2},{3,34},{35,3},{4,37},{36... | collective-permute-start | bytes 196616 | tf_op jit(solution)/shard_map/ppermute | solution.py:234
  25.2 5.8 %collective-permute-start.7 = (bf16[64,512]{1,0:T(8,128)(2,1)S(1)}, bf16[64,512]{1,0:T(8,128)(2,1)S(1)}, u32[]{:S(2)}, u32[]{:S(2)}) collective-permute-start(bf16[64,512]{1,0:T(8,128)(2,1)S(1)} %bitcast.38), channel_id=1, source_target_pairs={{0,1},{32,33},{1,0},{33,32},{2,3},{34,35},{3,2},{35,34},{4,5},{36,... | collective-permute-start | bytes 196616 | tf_op jit(solution)/shard_map/ppermute | solution.py:234
  25.8 5.8 %collective-permute-start.8 = (bf16[64,512]{1,0:T(8,128)(2,1)S(1)}, bf16[64,512]{1,0:T(8,128)(2,1)S(1)}, u32[]{:S(2)}, u32[]{:S(2)}) collective-permute-start(bf16[64,512]{1,0:T(8,128)(2,1)S(1)} %bitcast.39), channel_id=1, source_target_pairs={{0,32},{32,1},{1,33},{33,0},{2,34},{34,3},{3,35},{35,2},{4,36},{36... | collective-permute-start | bytes 196616 | tf_op jit(solution)/shard_map/ppermute | solution.py:234
  27.1 8.2 %collective-permute-start.1 = (bf16[80,512]{1,0:T(8,128)(2,1)S(1)}, bf16[80,512]{1,0:T(8,128)(2,1)S(1)}, u32[]{:S(2)}, u32[]{:S(2)}) collective-permute-start(bf16[80,512]{1,0:T(8,128)(2,1)S(1)} %get-tuple-element.41), channel_id=1, source_target_pairs={{0,128},{64,192},{128,0},{192,64},{1,129},{65,193},{129,1},{193,65... | collective-permute-start | bytes 245768 | tf_op jit(solution)/shard_map/ppermute | solution.py:232
  31.7 23.0 %copy-start.14 = (bf16[4,64,512]{2,1,0:T(8,128)(2,1)}, bf16[4,64,512]{2,1,0:T(8,128)(2,1)S(1)}, u32[]{:S(2)}) copy-start(bf16[4,64,512]{2,1,0:T(8,128)(2,1)S(1)} %pad_maximum_fusion.2.refs_4_) | copy-start | bytes 786436
  31.7 12.5 %collective-permute-start.10 = (bf16[4,64,512]{2,1,0:T(8,128)(2,1)S(1)}, bf16[4,64,512]{2,1,0:T(8,128)(2,1)S(1)}, u32[]{:S(2)}, u32[]{:S(2)}) collective-permute-start(bf16[4,64,512]{2,1,0:T(8,128)(2,1)S(1)} %pad_maximum_fusion.2.refs_4_), channel_id=1, source_target_pairs={{0,128},{64,192},{128,0},{192,64},{1,129},{65,193},{129,1},{193,65... | collective-permute-start | bytes 786440 | tf_op jit(solution)/shard_map/ppermute | solution.py:232
  33.2 7.9 %collective-permute-start.2 = (bf16[80,512]{1,0:T(8,128)(2,1)S(1)}, bf16[80,512]{1,0:T(8,128)(2,1)S(1)}, u32[]{:S(2)}, u32[]{:S(2)}) collective-permute-start(bf16[80,512]{1,0:T(8,128)(2,1)S(1)} %get-tuple-element.41), channel_id=1, source_target_pairs={{0,64},{64,128},{128,192},{192,0},{1,65},{65,129},{129,193},{193,1... | collective-permute-start | bytes 245768 | tf_op jit(solution)/shard_map/ppermute | solution.py:232
  35.3 5.8 %collective-permute-start = (bf16[80,512]{1,0:T(8,128)(2,1)S(1)}, bf16[80,512]{1,0:T(8,128)(2,1)S(1)}, u32[]{:S(2)}, u32[]{:S(2)}) collective-permute-start(bf16[80,512]{1,0:T(8,128)(2,1)S(1)} %get-tuple-element.41), channel_id=1, source_target_pairs={{0,192},{64,0},{128,64},{192,128},{1,193},{65,1},{129,65},{193,129... | collective-permute-start | bytes 245768 | tf_op jit(solution)/shard_map/ppermute | solution.py:232
  35.3 9.6 %collective-permute-start.11 = (bf16[4,64,512]{2,1,0:T(8,128)(2,1)S(1)}, bf16[4,64,512]{2,1,0:T(8,128)(2,1)S(1)}, u32[]{:S(2)}, u32[]{:S(2)}) collective-permute-start(bf16[4,64,512]{2,1,0:T(8,128)(2,1)S(1)} %pad_maximum_fusion.2.refs_4_), channel_id=1, source_target_pairs={{0,64},{64,128},{128,192},{192,0},{1,65},{65,129},{129,193},{193,1... | collective-permute-start | bytes 786440 | tf_op jit(solution)/shard_map/ppermute | solution.py:232
  41.2 12.8 %collective-permute-start.3 = (bf16[4,80,512]{2,1,0:T(8,128)(2,1)S(1)}, bf16[4,80,512]{2,1,0:T(8,128)(2,1)S(1)}, u32[]{:S(2)}, u32[]{:S(2)}) collective-permute-start(bf16[4,80,512]{2,1,0:T(8,128)(2,1)S(1)} %pad_maximum_fusion.1.refs_0_), channel_id=1, source_target_pairs={{0,33},{32,0},{1,32},{33,1},{2,35},{34,2},{3,34},{35,3},{4,37},{36... | collective-permute-start | bytes 983048 | tf_op jit(solution)/shard_map/ppermute | solution.py:234
  42.5 12.2 %collective-permute-start.4 = (bf16[4,80,512]{2,1,0:T(8,128)(2,1)S(1)}, bf16[4,80,512]{2,1,0:T(8,128)(2,1)S(1)}, u32[]{:S(2)}, u32[]{:S(2)}) collective-permute-start(bf16[4,80,512]{2,1,0:T(8,128)(2,1)S(1)} %pad_maximum_fusion.1.refs_0_), channel_id=1, source_target_pairs={{0,1},{32,33},{1,0},{33,32},{2,3},{34,35},{3,2},{35,34},{4,5},{36,... | collective-permute-start | bytes 983048 | tf_op jit(solution)/shard_map/ppermute | solution.py:234
  45.0 10.5 %collective-permute-start.5 = (bf16[4,80,512]{2,1,0:T(8,128)(2,1)S(1)}, bf16[4,80,512]{2,1,0:T(8,128)(2,1)S(1)}, u32[]{:S(2)}, u32[]{:S(2)}) collective-permute-start(bf16[4,80,512]{2,1,0:T(8,128)(2,1)S(1)} %pad_maximum_fusion.1.refs_0_), channel_id=1, source_target_pairs={{0,32},{32,1},{1,33},{33,0},{2,34},{34,3},{3,35},{35,2},{4,36},{36... | collective-permute-start | bytes 983048 | tf_op jit(solution)/shard_map/ppermute | solution.py:234
  45.7 7.6 %collective-permute-start.9 = (bf16[4,64,512]{2,1,0:T(8,128)(2,1)S(1)}, bf16[4,64,512]{2,1,0:T(8,128)(2,1)S(1)}, u32[]{:S(2)}, u32[]{:S(2)}) collective-permute-start(bf16[4,64,512]{2,1,0:T(8,128)(2,1)S(1)} %pad_maximum_fusion.2.refs_4_), channel_id=1, source_target_pairs={{0,192},{64,0},{128,64},{192,128},{1,193},{65,1},{129,65},{193,129... | collective-permute-start | bytes 786440 | tf_op jit(solution)/shard_map/ppermute | solution.py:232
  75.8 8.4 %collective-permute-start.13 = (f32[1024,512]{1,0:T(8,128)}, f32[1024,512]{1,0:T(8,128)}, u32[]{:S(2)}, u32[]{:S(2)}) collective-permute-start(f32[1024,512]{1,0:T(8,128)} %grad.2), channel_id=1, source_target_pairs={{0,2},{2,0},{1,3},{3,1},{4,6},{6,4},{5,7},{7,5},{8,10},{10,8},{9,1... | collective-permute-start | bytes 6291464 | tf_op jit(solution)/shard_map/ppermute | solution.py:238
  84.2 8.6 %copy-start.2 = (bf16[1024,2048]{1,0:T(8,128)(2,1)S(1)}, bf16[1024,2048]{1,0:T(8,128)(2,1)}, u32[]{:S(2)}) copy-start(bf16[1024,2048]{1,0:T(8,128)(2,1)} %copy-done.1) | copy-start | bytes 12582916
  92.5 9.3 %copy-start.6 = (f32[1024,512]{1,0:T(8,128)}, f32[1024,512]{1,0:T(8,128)S(1)}, u32[]{:S(2)}) copy-start(f32[1024,512]{1,0:T(8,128)S(1)} %get-tuple-element.18.refs_3_) | copy-start | bytes 6291460
  92.5 9.3 %copy-start.10 = (f32[1024,512]{1,0:T(8,128)}, f32[1024,512]{1,0:T(8,128)S(1)}, u32[]{:S(2)}) copy-start(f32[1024,512]{1,0:T(8,128)S(1)} %get-tuple-element.20.refs_5_) | copy-start | bytes 6291460
  92.5 19.8 %copy-start.12 = (bf16[1024,512]{1,0:T(8,128)(2,1)}, bf16[1024,512]{1,0:T(8,128)(2,1)S(1)}, u32[]{:S(2)}) copy-start(bf16[1024,512]{1,0:T(8,128)(2,1)S(1)} %get-tuple-element.17.wb_ref.wb_own) | copy-start | bytes 3145732
  92.5 26.2 %collective-permute-start.14 = (bf16[1024,512]{1,0:T(8,128)(2,1)S(1)}, bf16[1024,512]{1,0:T(8,128)(2,1)S(1)}, u32[]{:S(2)}, u32[]{:S(2)}) collective-permute-start(bf16[1024,512]{1,0:T(8,128)(2,1)S(1)} %get-tuple-element.17.wb_ref.wb_own), channel_id=1, source_target_pairs={{0,2},{2,0},{1,3},{3,1},{4,6},{6,4},{5,7},{7,5},{8,10},{10,8},{9,1... | collective-permute-start | bytes 3145736 | tf_op jit(solution)/shard_map/ppermute | solution.py:238
  101.9 10.1 %collective-permute-start.16 = (bf16[256,512]{1,0:T(8,128)(2,1)S(1)}, bf16[256,512]{1,0:T(8,128)(2,1)S(1)}, u32[]{:S(2)}, u32[]{:S(2)}) collective-permute-start(bf16[256,512]{1,0:T(8,128)(2,1)S(1)} %get-tuple-element.28), channel_id=1, source_target_pairs={{0,32},{32,1},{1,33},{33,0},{2,34},{34,3},{3,35},{35,2},{4,36},{36... | collective-permute-start | bytes 786440 | tf_op jit(solution)/shard_map/ppermute | solution.py:234
  103.6 8.5 %collective-permute-start.17 = (bf16[256,512]{1,0:T(8,128)(2,1)S(1)}, bf16[256,512]{1,0:T(8,128)(2,1)S(1)}, u32[]{:S(2)}, u32[]{:S(2)}) collective-permute-start(bf16[256,512]{1,0:T(8,128)(2,1)S(1)} %get-tuple-element.29), channel_id=1, source_target_pairs={{0,33},{32,0},{1,32},{33,1},{2,35},{34,2},{3,34},{35,3},{4,37},{36... | collective-permute-start | bytes 786440 | tf_op jit(solution)/shard_map/ppermute | solution.py:234
  129.3 10.6 %collective-permute-start.21 = (bf16[256,512]{1,0:T(8,128)(2,1)S(1)}, bf16[256,512]{1,0:T(8,128)(2,1)S(1)}, u32[]{:S(2)}, u32[]{:S(2)}) collective-permute-start(bf16[256,512]{1,0:T(8,128)(2,1)S(1)} %get-tuple-element.30), channel_id=1, source_target_pairs={{0,32},{32,1},{1,33},{33,0},{2,34},{34,3},{3,35},{35,2},{4,36},{36... | collective-permute-start | bytes 786440 | tf_op jit(solution)/shard_map/ppermute | solution.py:234
  130.6 11.3 %collective-permute-start.22 = (bf16[256,512]{1,0:T(8,128)(2,1)S(1)}, bf16[256,512]{1,0:T(8,128)(2,1)S(1)}, u32[]{:S(2)}, u32[]{:S(2)}) collective-permute-start(bf16[256,512]{1,0:T(8,128)(2,1)S(1)} %get-tuple-element.31), channel_id=1, source_target_pairs={{0,33},{32,0},{1,32},{33,1},{2,35},{34,2},{3,34},{35,3},{4,37},{36... | collective-permute-start | bytes 786440 | tf_op jit(solution)/shard_map/ppermute | solution.py:234
  136.4 41.0 %collective-permute-start.15 = (f32[1024,512]{1,0:T(8,128)}, f32[1024,512]{1,0:T(8,128)}, u32[]{:S(2)}, u32[]{:S(2)}) collective-permute-start(f32[1024,512]{1,0:T(8,128)} %grad.3), channel_id=1, source_target_pairs={{0,2},{2,0},{1,3},{3,1},{4,6},{6,4},{5,7},{7,5},{8,10},{10,8},{9,1... | collective-permute-start | bytes 6291464 | tf_op jit(solution)/shard_map/ppermute | solution.py:238
  136.4 8.4 %collective-permute-start.18 = (bf16[128,512]{1,0:T(8,128)(2,1)S(1)}, bf16[128,512]{1,0:T(8,128)(2,1)S(1)}, u32[]{:S(2)}, u32[]{:S(2)}) collective-permute-start(bf16[128,512]{1,0:T(8,128)(2,1)S(1)} %get-tuple-element.32), channel_id=1, source_target_pairs={{0,64},{64,128},{128,192},{192,0},{1,65},{65,129},{129,193},{193,1... | collective-permute-start | bytes 393224 | tf_op jit(solution)/shard_map/ppermute | solution.py:232
  138.1 9.9 %collective-permute-start.19 = (bf16[128,512]{1,0:T(8,128)(2,1)S(1)}, bf16[128,512]{1,0:T(8,128)(2,1)S(1)}, u32[]{:S(2)}, u32[]{:S(2)}) collective-permute-start(bf16[128,512]{1,0:T(8,128)(2,1)S(1)} %get-tuple-element.34), channel_id=1, source_target_pairs={{0,192},{64,0},{128,64},{192,128},{1,193},{65,1},{129,65},{193,129... | collective-permute-start | bytes 393224 | tf_op jit(solution)/shard_map/ppermute | solution.py:232
  139.9 10.2 %collective-permute-start.20 = (bf16[128,512]{1,0:T(8,128)(2,1)S(1)}, bf16[128,512]{1,0:T(8,128)(2,1)S(1)}, u32[]{:S(2)}, u32[]{:S(2)}) collective-permute-start(bf16[128,512]{1,0:T(8,128)(2,1)S(1)} %get-tuple-element.33), channel_id=1, source_target_pairs={{0,128},{64,192},{128,0},{192,64},{1,129},{65,193},{129,1},{193,65... | collective-permute-start | bytes 393224 | tf_op jit(solution)/shard_map/ppermute | solution.py:232
  142.1 8.1 %collective-permute-start.23 = (bf16[128,512]{1,0:T(8,128)(2,1)S(1)}, bf16[128,512]{1,0:T(8,128)(2,1)S(1)}, u32[]{:S(2)}, u32[]{:S(2)}) collective-permute-start(bf16[128,512]{1,0:T(8,128)(2,1)S(1)} %get-tuple-element.35), channel_id=1, source_target_pairs={{0,64},{64,128},{128,192},{192,0},{1,65},{65,129},{129,193},{193,1... | collective-permute-start | bytes 393224 | tf_op jit(solution)/shard_map/ppermute | solution.py:232
  144.8 6.9 %collective-permute-start.24 = (bf16[128,512]{1,0:T(8,128)(2,1)S(1)}, bf16[128,512]{1,0:T(8,128)(2,1)S(1)}, u32[]{:S(2)}, u32[]{:S(2)}) collective-permute-start(bf16[128,512]{1,0:T(8,128)(2,1)S(1)} %get-tuple-element.37), channel_id=1, source_target_pairs={{0,192},{64,0},{128,64},{192,128},{1,193},{65,1},{129,65},{193,129... | collective-permute-start | bytes 393224 | tf_op jit(solution)/shard_map/ppermute | solution.py:232
  148.1 6.5 %collective-permute-start.25 = (bf16[128,512]{1,0:T(8,128)(2,1)S(1)}, bf16[128,512]{1,0:T(8,128)(2,1)S(1)}, u32[]{:S(2)}, u32[]{:S(2)}) collective-permute-start(bf16[128,512]{1,0:T(8,128)(2,1)S(1)} %get-tuple-element.36), channel_id=1, source_target_pairs={{0,128},{64,192},{128,0},{192,64},{1,129},{65,193},{129,1},{193,65... | collective-permute-start | bytes 393224 | tf_op jit(solution)/shard_map/ppermute | solution.py:232
  (23 other events, 48.1 us)
